TPU v7x, 512 devices: a whole 4x8x8 slice. The times are simulated.
512 devices in a mesh: row: 32 (over y_hi, z, core), col: 4 (over y_lo), dp: 4 (over x).
Axes of the slice: x: 4, y: 8 (y_hi: 2, y_lo: 4; y = y_hi * 4 + y_lo), z: 8, core: 2. Of those that a mesh axis runs over, the one named last changes fastest.
Arguments:
- activations: bfloat16 [2048, 8192], P('dp', 'row'), may hold values from -6 to 6
- out_grads: bfloat16 [2048, 14336], P('dp', 'col'), may hold values from -0.5390625 to 0.5390625
- projector: bfloat16 [8192, 256], P('row'), may hold values from -0.125 to 0.125
- weight: bfloat16 [8192, 14336], P('row', ('col', 'dp')), may hold values from -6 to 6
- moment: float32 [256, 14336], P('row', ('col', 'dp')), may hold values from -1.8 to 1.8
- second: float32 [256, 14336], P('row', ('col', 'dp')), may hold values from 0.0001 to 0.01
Outputs:
- new_weight: bfloat16 [8192, 14336], P('row', ('col', 'dp'))
- new_moment: float32 [256, 14336], P('row', ('col', 'dp'))
- new_second: float32 [256, 14336], P('row', ('col', 'dp'))
All inputs are finite; a program needn't handle non-finite values.
Results may differ from a plain program's by a relative error of at most 0.0034.
Values may be sent and summed in bfloat16 or wider, within the bound.
A program may use at most 64 MiB of HBM per device.

v0:
```python
import jax
import jax.numpy as jnp
from jax import lax
from jax.sharding import PartitionSpec as P


def contract_first(left, right):
    return lax.dot_general(
        left,
        right,
        (((0,), (0,)), ((), ())),
        precision=lax.Precision.HIGHEST,
        preferred_element_type=jnp.float32,
    )


def per_device(activations, out_grads, projector, weight, moment, second):
    gradient = lax.dot_general(
        activations, out_grads, (((0,), (0,)), ((), ())), preferred_element_type=jnp.float32
    )
    block = projector.astype(jnp.float32)
    partial_sum = lax.psum_scatter(
        contract_first(block, gradient), "row", scatter_dimension=0, tiled=True
    )
    low = lax.psum_scatter(partial_sum, "dp", scatter_dimension=1, tiled=True) * (
        1.0 / lax.axis_size("dp")
    )
    new_moment = 0.9 * moment + 0.1 * low
    new_second = 0.999 * second + 0.001 * low * low
    first_fix = 1.0 / (1.0 - 0.9**10)
    second_fix = 1.0 / (1.0 - 0.999**10)
    direction = (new_moment * first_fix / (jnp.sqrt(new_second * second_fix) + 1e-08)).astype(
        jnp.bfloat16
    )
    block = projector
    update = jnp.dot(
        block,
        lax.all_gather(direction, "row", axis=0, tiled=True),
        preferred_element_type=jnp.float32,
    )
    new_weight = (weight.astype(jnp.float32) - 0.5 * update).astype(jnp.bfloat16)
    return (new_weight, new_moment, new_second)


def solution(mesh):
    in_specs = (
        P("dp", "row"),
        P("dp", "col"),
        P("row", None),
        P("row", ("col", "dp")),
        P("row", ("col", "dp")),
        P("row", ("col", "dp")),
    )
    out_specs = (P("row", ("col", "dp")), P("row", ("col", "dp")), P("row", ("col", "dp")))
    return jax.shard_map(
        per_device, mesh=mesh, in_specs=in_specs, out_specs=out_specs, check_vma=False
    )
```

profile of v0, /device:TPU:1, one launch (start us, length us, event | category | flops | bytes accessed | tf_op | source)
XLA Modules:
  0.0 263.2 jit_solution(7578075182394808620)
XLA Ops:
  7.2 0.0 copy-start
  7.2 0.0 copy-start.1
  7.2 0.0 reduce-scatter.7.cloned.1.call-start
  7.2 0.9 copy-done
  8.1 3.2 %fusion.3 = f32[256,3584]{1,0:T(8,128)S(1)} fusion(bf16[512,256]{1,0:T(8,128)(2,1)S(1)} %copy-done, bf16[512,3584]{1,0:T(8,128)(2,1)} %param.7), kind=kOutput, calls=%fused_computation.8 | convolution fusion | flops 939524096 | bytes 7602176 | tf_op jit(solution)/shard_map/dot_general | solution.py:18
  11.3 0.0 copy-done.1
  11.3 4.9 %convolution_bitcast_fusion = f32[256,3584]{0,1:T(8,128)} fusion(f32[256,3584]{1,0:T(8,128)S(1)} %fusion.3, bf16[256,256]{1,0:T(8,128)(2,1)S(1)} %copy-done.1), kind=kOutput, calls=%fused_computation | convolution fusion | flops 2818572288 | bytes 7471104 | tf_op jit(solution)/shard_map/dot_general | solution.py:8
  16.2 5.2 %copy.30 = f32[256,3584]{1,0:T(8,128)} copy(f32[256,3584]{0,1:T(8,128)} %convolution_bitcast_fusion) | data formatting | bytes 7340032
  21.4 0.0 copy-start.2
  21.4 0.0 copy-start.3
  21.4 0.0 copy-start.4
  21.4 0.0 reduce-scatter.7.cloned.1.call-update
  21.4 0.0 reduce-scatter.5.cloned.1.call-start
  21.4 146.8 %reduce-scatter.7.cloned.1.call-done = f32[8,3584]{1,0:T(8,128)} async-done(((f32[256,3584]{1,0:T(8,128)}), f32[8,3584]{1,0:T(8,128)}) %reduce-scatter.7.cloned.1.call-update) | async-done | bytes 114704 | tf_op jit(solution)/shard_map/reduce_scatter | solution.py:22
  168.2 0.0 reduce-scatter.5.cloned.1.call-update
  168.2 0.0 copy-done.2
  168.2 0.2 copy.27
  168.4 26.4 %reduce-scatter.5.cloned.1.call-done = f32[8,896]{1,0:T(8,128)} async-done(((f32[8,3584]{1,0:T(8,128)}), f32[8,896]{1,0:T(8,128)}) %reduce-scatter.5.cloned.1.call-update) | async-done | bytes 28688 | tf_op jit(solution)/shard_map/reduce_scatter | solution.py:25
  194.8 0.0 copy-done.3
  194.8 0.0 copy-done.4
  194.8 1.4 divide_convert_fusion
  196.2 58.9 %all_gather.3 = bf16[256,896]{1,0:T(8,128)(2,1)S(1)} all-gather(bf16[8,896]{1,0:T(8,128)(2,1)S(1)} %get-tuple-element.12), channel_id=1, replica_groups=mesh['row'=32,'col'=4,'dp'=4] {'row'}, dimensions={0}, use_global_device_ids=true | all-gather | bytes 473088 | tf_op jit(solution)/shard_map/all_gather | solution.py:38
  255.1 0.3 fusion.2
  255.4 1.0 copy.29
Async XLA Ops:
  7.2 1.0 copy-start
  7.2 4.1 %copy-start.1 = (bf16[256,256]{1,0:T(8,128)(2,1)S(1)}, bf16[256,256]{1,0:T(8,128)(2,1)}, u32[]{:S(2)}) copy-start(bf16[256,256]{1,0:T(8,128)(2,1)} %param.8) | copy-start | bytes 393220
  7.2 161.0 %reduce-scatter.7.cloned.1.call-start = ((), (), s32[]{:S(2)}) async-start(), calls=%async_computation.3 | async-start | bytes 3784704 | tf_op jit(solution)/shard_map/reduce_scatter | solution.py:22
  21.4 146.9 %copy-start.2 = (bf16[256,896]{1,0:T(8,128)(2,1)S(1)}, bf16[256,896]{1,0:T(8,128)(2,1)}, u32[]{:S(2)}) copy-start(bf16[256,896]{1,0:T(8,128)(2,1)} %param.9) | copy-start | bytes 1376260
  21.4 173.5 %copy-start.3 = (f32[8,896]{1,0:T(8,128)S(1)}, f32[8,896]{1,0:T(8,128)}, u32[]{:S(2)}) copy-start(f32[8,896]{1,0:T(8,128)} %param.10) | copy-start | bytes 86020
  21.4 173.5 %copy-start.4 = (f32[8,896]{1,0:T(8,128)S(1)}, f32[8,896]{1,0:T(8,128)}, u32[]{:S(2)}) copy-start(f32[8,896]{1,0:T(8,128)} %param.11) | copy-start | bytes 86020
  21.4 173.4 %reduce-scatter.5.cloned.1.call-start = ((), (), s32[]{:S(2)}) async-start(), calls=%async_computation.2 | async-start | bytes 143360 | tf_op jit(solution)/shard_map/reduce_scatter | solution.py:25
Sparse Core Ops, SparseCore 0:
  21.5 146.6 reduce-scatter.6
  171.0 23.7 reduce-scatter.4
where the time goes:
time: 264 us; the launch traced here: 263 us
  waiting for transfers between devices  173 us (66%)
  blocking collectives  58.9 us (22%)
  between operations  14.1 us (5%)
  matrix products  8.39 us (3%)
  local copies, waits for them, and re-layouts  7.27 us (3%)
    reduce_scatter x1, waiting for transfers between devices, per_device(): lax.psum_scatter(contract_first(block, gradient), 'row', scatter_dimensio...  147 us
    all_gather x1, blocking collectives, per_device(): lax.all_gather(direction, 'row', axis=0, tiled=True)  58.9 us
    reduce_scatter x1, waiting for transfers between devices, per_device(): lax.psum_scatter(partial_sum, 'dp', scatter_dimension=1, tiled=True)  26.4 us
    unnamed x13, local copies, waits for them, and re-layouts  7.27 us
  transfers between devices with their start and end apart: 2, of which 2 were waited for; matrix products, arithmetic and copies ran while one was open for 0% of the time, Pallas kernels for 0%

commit v1 on v0

v1 whole, which is shorter than its diff:
```python
import jax
import jax.numpy as jnp
from jax import lax
from jax.experimental import pallas as pl
from jax.experimental.pallas import tpu as pltpu
from jax.sharding import PartitionSpec as P

MESH = pl.DeviceIdType.MESH
A_TYPE = jnp.float32
D_TYPE = jnp.float32

NZ, NK, NYH, NYL, NX = 8, 2, 2, 4, 4
NQ, NY = NZ * NK, NYH * NYL
OWN = 8
TOK = 128
R = 256
COLS = 896
FAR_FIRST = (4, 3, 5, 2, 6, 1, 7)
NEAR_FIRST = (1, 7, 2, 6, 3, 5, 4)
FIRST_FIX = 1.0 / (1.0 - 0.9**10)
SECOND_FIX = 1.0 / (1.0 - 0.999**10)


def kernel(
    act, grads, proj, weight, moment, second,
    new_weight, new_moment, new_second,
    act_v, proj_v, perm_v, grads_v, weight_v, mv, state_v, out_v,
    send_a, recv_a, recv_b, send_d, recv_d, dirs, low_v,
    in_sem, out_sem, mv_sem, a_sem, b_sem, d_sem, f_sem, c_sem,
):
    row, col, dp = lax.axis_index("row"), lax.axis_index("col"), lax.axis_index("dp")
    yh, z, k = row // NQ, (row // NK) % NZ, row % NK
    y, q = yh * NYL + col, row % NQ

    def at_zk(dz, dk):
        return (yh * NQ + ((z + dz) % NZ) * NK + (k + dk) % NK, col, dp)

    def at_y(dy):
        to = (y + dy) % NY
        return ((to // NYL) * NQ + q, to % NYL, dp)

    def at_x(dx):
        return (row, col, (dp + dx) % NX)

    zk = [(dz, dk) for dz in FAR_FIRST for dk in range(NK)] + [(0, 1)]

    loads = [
        pltpu.make_async_copy(act.at[pl.ds(pl.multiple_of(col * TOK, TOK), TOK), :], act_v, in_sem.at[0]),
        pltpu.make_async_copy(proj, proj_v, in_sem.at[1]),
        pltpu.make_async_copy(moment, mv.at[yh, 0], in_sem.at[2]),
        pltpu.make_async_copy(second, mv.at[yh, 1], in_sem.at[3]),
    ]
    for x in range(NX):
        loads.append(pltpu.make_async_copy(grads.at[:, pl.ds(x * COLS, COLS)], grads_v.at[x], in_sem.at[4 + x]))
    loads.append(pltpu.make_async_copy(weight, weight_v, in_sem.at[8]))
    for load in loads[:2]:
        load.start()

    barrier = pltpu.get_barrier_semaphore()
    peers = [at_zk(dz, dk) for dz, dk in zk] + [at_y(dy) for dy in FAR_FIRST] + [at_x(dx) for dx in (2, 1, 3)]
    for peer in peers:
        pl.semaphore_signal(barrier, inc=1, device_id=peer, device_id_type=MESH)
    for load in loads[2:]:
        load.start()

    loads[0].wait()
    loads[1].wait()
    part = lax.dot_general(proj_v[...], act_v[...], (((0,), (1,)), ((), ())), preferred_element_type=jnp.float32)
    part = part.reshape(NYH, NQ, OWN, TOK)
    send_a[...] = jnp.concatenate([part[0], part[1]], axis=1).astype(A_TYPE)

    pl.semaphore_wait(barrier, len(peers))
    copies = []

    sends_a = []
    for j, (dz, dk) in enumerate(zk):
        to = ((z + dz) % NZ) * NK + (k + dk) % NK
        copy = pltpu.make_async_remote_copy(
            src_ref=send_a.at[to], dst_ref=recv_a.at[j], send_sem=a_sem.at[0, j], recv_sem=a_sem.at[1, j],
            device_id=at_zk(dz, dk), device_id_type=MESH,
        )
        copy.start()
        sends_a.append(copy)

    loads[2].wait()
    loads[3].wait()
    send_mv = pltpu.make_async_remote_copy(
        src_ref=mv.at[yh], dst_ref=mv.at[yh], send_sem=mv_sem.at[0], recv_sem=mv_sem.at[1],
        device_id=at_y(NYL), device_id_type=MESH,
    )
    send_mv.start()

    source = lax.broadcasted_iota(jnp.int32, (R, R), 0)
    place = lax.broadcasted_iota(jnp.int32, (R, R), 1)
    wanted = (place % (NYH * OWN)) // OWN * (NQ * OWN) + place // (NYH * OWN) * OWN + place % OWN
    shuffle = jnp.where(source == wanted, 1.0, 0.0).astype(jnp.bfloat16)
    perm_v[...] = jnp.dot(proj_v[...], shuffle, preferred_element_type=jnp.float32).astype(jnp.bfloat16)

    total = send_a[q].astype(jnp.float32)
    for j in reversed(range(len(zk))):
        sends_a[j].wait_recv()
        total += recv_a[j].astype(jnp.float32)

    recv_b[y] = total
    sends_b = []
    for j, dy in enumerate(FAR_FIRST):
        copy = pltpu.make_async_remote_copy(
            src_ref=recv_b.at[y], dst_ref=recv_b.at[y], send_sem=b_sem.at[0, j], recv_sem=b_sem.at[1, j],
            device_id=at_y(dy), device_id_type=MESH,
        )
        copy.start()
        sends_b.append(copy)
    for load in loads[4:8]:
        load.wait()
    for copy in sends_b:
        copy.wait_recv()
    coords = jnp.concatenate([recv_b[c] + recv_b[NYL + c] for c in range(NYL)], axis=1)
    high = coords.astype(jnp.bfloat16)
    rest = (coords - high.astype(jnp.float32)).astype(jnp.bfloat16)
    both = jnp.concatenate([high, rest], axis=0)

    def low_of(to):
        product = jnp.dot(both, grads_v[to], preferred_element_type=jnp.float32)
        return product[: NYH * OWN] + product[NYH * OWN :]

    sends_d = []
    for j, dx in enumerate((2, 1, 3)):
        send_d[j] = low_of((dp + dx) % NX).astype(D_TYPE)
        copy = pltpu.make_async_remote_copy(
            src_ref=send_d.at[j], dst_ref=recv_d.at[j], send_sem=d_sem.at[0, j], recv_sem=d_sem.at[1, j],
            device_id=at_x(dx), device_id_type=MESH,
        )
        copy.start()
        sends_d.append(copy)
    low_v[...] = low_of(dp)
    send_mv.wait_recv()
    for copy in sends_d:
        copy.wait_recv()
    low = low_v[...] + recv_d[1].astype(jnp.float32) + recv_d[2].astype(jnp.float32) + recv_d[0].astype(jnp.float32)
    low = (low * (1.0 / NX)).reshape(NYH, OWN, COLS)
    state_m = 0.9 * mv[:, 0] + 0.1 * low
    state_s = 0.999 * mv[:, 1] + 0.001 * low * low
    direction = state_m * FIRST_FIX / (jnp.sqrt(state_s * SECOND_FIX) + 1e-08)
    dirs[q] = direction.reshape(NYH * OWN, COLS).astype(jnp.bfloat16)

    sends_f = []
    for j, dz in enumerate(FAR_FIRST):
        copy = pltpu.make_async_remote_copy(
            src_ref=dirs.at[q], dst_ref=dirs.at[q], send_sem=f_sem.at[0, j], recv_sem=f_sem.at[1, j],
            device_id=at_zk(dz, 0), device_id_type=MESH,
        )
        copy.start()
        sends_f.append(copy)

    def to_other_core(block, j):
        copy = pltpu.make_async_remote_copy(
            src_ref=dirs.at[block], dst_ref=dirs.at[block], send_sem=c_sem.at[0, j], recv_sem=c_sem.at[1, j],
            device_id=at_zk(0, 1), device_id_type=MESH,
        )
        copy.start()
        return copy

    sends_c = [to_other_core(q, 0)]
    state_v[0] = state_m
    state_v[1] = state_s
    stores = [
        pltpu.make_async_copy(state_v.at[0, yh], new_moment, out_sem.at[0]),
        pltpu.make_async_copy(state_v.at[1, yh], new_second, out_sem.at[1]),
    ]
    for store in stores:
        store.start()
    loads[8].wait()
    for j, dz in enumerate(NEAR_FIRST):
        sends_f[FAR_FIRST.index(dz)].wait_recv()
        sends_c.append(to_other_core(((z - dz + NZ) % NZ) * NK + k, 1 + j))
    for copy in sends_c:
        copy.wait_recv()

    update = jnp.dot(perm_v[...], dirs[...].reshape(R, COLS), preferred_element_type=jnp.float32)
    out_v[...] = (weight_v[...].astype(jnp.float32) - 0.5 * update).astype(jnp.bfloat16)
    store = pltpu.make_async_copy(out_v, new_weight, out_sem.at[2])
    store.start()
    for copy in sends_a + [send_mv] + sends_b + sends_d + sends_f + sends_c:
        copy.wait_send()
    for copy in stores + [store]:
        copy.wait()


def per_device(activations, out_grads, projector, weight, moment, second):
    any_space = pl.BlockSpec(memory_space=pl.ANY)
    return pl.pallas_call(
        kernel,
        out_shape=(
            jax.ShapeDtypeStruct(weight.shape, jnp.bfloat16),
            jax.ShapeDtypeStruct(moment.shape, jnp.float32),
            jax.ShapeDtypeStruct(second.shape, jnp.float32),
        ),
        in_specs=[any_space] * 6,
        out_specs=[any_space] * 3,
        scratch_shapes=[
            pltpu.VMEM((TOK, 256), jnp.bfloat16),
            pltpu.VMEM((256, R), jnp.bfloat16),
            pltpu.VMEM((256, R), jnp.bfloat16),
            pltpu.VMEM((NX, 512, COLS), jnp.bfloat16),
            pltpu.VMEM((256, COLS), jnp.bfloat16),
            pltpu.VMEM((NYH, 2, OWN, COLS), jnp.float32),
            pltpu.VMEM((2, NYH, OWN, COLS), jnp.float32),
            pltpu.VMEM((256, COLS), jnp.bfloat16),
            pltpu.VMEM((NQ, NYH * OWN, TOK), A_TYPE),
            pltpu.VMEM((NQ, NYH * OWN, TOK), A_TYPE),
            pltpu.VMEM((NY, NYH * OWN, TOK), jnp.float32),
            pltpu.VMEM((NX - 1, NYH * OWN, COLS), D_TYPE),
            pltpu.VMEM((NX - 1, NYH * OWN, COLS), D_TYPE),
            pltpu.VMEM((NQ, NYH * OWN, COLS), jnp.bfloat16),
            pltpu.VMEM((NYH * OWN, COLS), jnp.float32),
            pltpu.SemaphoreType.DMA((9,)),
            pltpu.SemaphoreType.DMA((3,)),
            pltpu.SemaphoreType.DMA((2,)),
            pltpu.SemaphoreType.DMA((2, NQ)),
            pltpu.SemaphoreType.DMA((2, NY)),
            pltpu.SemaphoreType.DMA((2, NX)),
            pltpu.SemaphoreType.DMA((2, NZ)),
            pltpu.SemaphoreType.DMA((2, NZ)),
        ],
        compiler_params=pltpu.CompilerParams(
            collective_id=0, has_side_effects=True, vmem_limit_bytes=60 * 1024 * 1024
        ),
        name="galore_step",
    )(activations, out_grads, projector, weight, moment, second)


def solution(mesh):
    in_specs = (
        P("dp", "row"),
        P("dp", "col"),
        P("row", None),
        P("row", ("col", "dp")),
        P("row", ("col", "dp")),
        P("row", ("col", "dp")),
    )
    out_specs = (P("row", ("col", "dp")), P("row", ("col", "dp")), P("row", ("col", "dp")))
    return jax.shard_map(
        per_device, mesh=mesh, in_specs=in_specs, out_specs=out_specs, check_vma=False
    )
```

time: 264 us -> 47.3 us (0.18)
  waiting for transfers between devices: 173 us -> 0 us
  blocking collectives: 58.9 us -> 0 us
  Pallas kernels: 0 us -> 41.8 us
  between operations: 14.1 us -> 0.64 us
  matrix products: 8.39 us -> 0 us
  local copies, waits for them, and re-layouts: 7.27 us -> 4.54 us
    reduce_scatter x2 -> x0, waiting for transfers between devices: 173 us -> none  [the longest x1 147 us: per_device(): lax.psum_scatter(contract_first(block, gradient), 'row', scatter_dimensio...]
    all_gather x1 -> x0, blocking collectives: 58.9 us -> none  [per_device(): lax.all_gather(direction, 'row', axis=0, tiled=True)]
    pallas_call x0 -> x1, Pallas kernels: none -> 41.8 us  [per_device(): pl.pallas_call(kernel, out_shape=(jax.ShapeDtypeStruct(weight.shape, jnp....]
    dot_general x3 -> x0, matrix products: 8.39 us -> none  [the longest x1 4.88 us: contract_first(): lax.dot_general(left, right, (((0,), (0,)), ((), ())), precision=lax.Prec...]
    unnamed x13 -> x3, local copies, waits for them, and re-layouts: 7.27 us -> 4.54 us
  transfers between devices with their start and end apart: 2 -> 0, of which waited for: 2 -> 0; matrix products, arithmetic and copies ran while one was open for 0% -> 0% of each run, Pallas kernels for 0% -> 0%
where the time goes in v1:
time: 47.3 us; the launch traced here: 47 us
  Pallas kernels  41.8 us (88%)
  local copies, waits for them, and re-layouts  4.54 us (10%)
  between operations  0.64 us (1%)
    pallas_call x1, Pallas kernels, per_device(): pl.pallas_call(kernel, out_shape=(jax.ShapeDtypeStruct(weight.shape, jnp....  41.8 us
    unnamed x3, local copies, waits for them, and re-layouts  4.54 us

profile of v1, /device:TPU:1, one launch (start us, length us, event | category | flops | bytes accessed | tf_op | source)
XLA Modules:
  0.0 47.0 jit_solution(18220108780241130307)
XLA Ops:
  0.6 41.8 %galore_step.1 = (bf16[256,896]{1,0:T(8,128)(2,1)}, f32[8,896]{1,0:T(8,128)}, f32[8,896]{1,0:T(8,128)}) custom-call(bf16[512,256]{1,0:T(8,128)(2,1)} %act.1, bf16[512,3584]{1,0:T(8,128)(2,1)} %grads.1, bf16[256,256]{1,0:T(8,128)(2,1)} %proj.1, bf16[256,896]{1,0:T(8,128)(2,1)} %weight.1, f32[8,896]{1,0:T(8,128)} %moment.1, f32[8,896]{1,0:T(8,128)} %second.1), custom_call_target="tpu_custom_call" | custom-call | tf_op jit(solution)/shard_map/galore_step/pallas_call | solution.py:191
  42.5 1.8 %copy.12 = bf16[256,896]{1,0:T(8,128)(2,1)} copy(bf16[256,896]{1,0:T(8,128)(2,1)} %get-tuple-element.6) | data formatting | bytes 917504
  44.3 1.4 %copy.13 = f32[8,896]{1,0:T(8,128)} copy(f32[8,896]{1,0:T(8,128)} %get-tuple-element.7) | data formatting | bytes 57344
  45.6 1.4 %copy.14 = f32[8,896]{1,0:T(8,128)} copy(f32[8,896]{1,0:T(8,128)} %get-tuple-element.8) | data formatting | bytes 57344

commit v2 on v1

--- a/solution.py
+++ b/solution.py
@@ -23,10 +23,9 @@
 
 def kernel(
     act, grads, proj, weight, moment, second,
-    new_weight, new_moment, new_second,
-    act_v, proj_v, perm_v, grads_v, weight_v, mv, state_v, out_v,
-    send_a, recv_a, recv_b, send_d, recv_d, dirs, low_v,
-    in_sem, out_sem, mv_sem, a_sem, b_sem, d_sem, f_sem, c_sem,
+    dirs, perm_v, weight_v, state_v,
+    act_v, proj_v, grads_v, mv, send_a, recv_a, recv_b, send_d, recv_d, low_v,
+    in_sem, mv_sem, a_sem, b_sem, d_sem, f_sem, c_sem,
 ):
     row, col, dp = lax.axis_index("row"), lax.axis_index("col"), lax.axis_index("dp")
     yh, z, k = row // NQ, (row // NK) % NZ, row % NK
@@ -161,14 +160,8 @@
         return copy
 
     sends_c = [to_other_core(q, 0)]
-    state_v[0] = state_m
-    state_v[1] = state_s
-    stores = [
-        pltpu.make_async_copy(state_v.at[0, yh], new_moment, out_sem.at[0]),
-        pltpu.make_async_copy(state_v.at[1, yh], new_second, out_sem.at[1]),
-    ]
-    for store in stores:
-        store.start()
+    state_v[0] = jnp.where(yh == 0, state_m[0], state_m[1])
+    state_v[1] = jnp.where(yh == 0, state_s[0], state_s[1])
     loads[8].wait()
     for j, dz in enumerate(NEAR_FIRST):
         sends_f[FAR_FIRST.index(dz)].wait_recv()
@@ -176,45 +169,50 @@
     for copy in sends_c:
         copy.wait_recv()
 
-    update = jnp.dot(perm_v[...], dirs[...].reshape(R, COLS), preferred_element_type=jnp.float32)
-    out_v[...] = (weight_v[...].astype(jnp.float32) - 0.5 * update).astype(jnp.bfloat16)
-    store = pltpu.make_async_copy(out_v, new_weight, out_sem.at[2])
-    store.start()
     for copy in sends_a + [send_mv] + sends_b + sends_d + sends_f + sends_c:
         copy.wait_send()
-    for copy in stores + [store]:
-        copy.wait()
+
+
+def finish(dirs, perm, weight, state, new_weight, new_moment, new_second, out_v, out_sem):
+    stores = [
+        pltpu.make_async_copy(state.at[0], new_moment, out_sem.at[0]),
+        pltpu.make_async_copy(state.at[1], new_second, out_sem.at[1]),
+    ]
+    for store in stores:
+        store.start()
+    update = jnp.dot(perm[...], dirs[...].reshape(R, COLS), preferred_element_type=jnp.float32)
+    out_v[...] = (weight[...].astype(jnp.float32) - 0.5 * update).astype(jnp.bfloat16)
+    stores.append(pltpu.make_async_copy(out_v, new_weight, out_sem.at[2]))
+    stores[2].start()
+    for store in stores:
+        store.wait()
 
 
 def per_device(activations, out_grads, projector, weight, moment, second):
     any_space = pl.BlockSpec(memory_space=pl.ANY)
-    return pl.pallas_call(
+    vmem = pl.BlockSpec(memory_space=pltpu.VMEM)
+    held = pl.pallas_call(
         kernel,
         out_shape=(
-            jax.ShapeDtypeStruct(weight.shape, jnp.bfloat16),
-            jax.ShapeDtypeStruct(moment.shape, jnp.float32),
-            jax.ShapeDtypeStruct(second.shape, jnp.float32),
+            pltpu.VMEM((NQ, NYH * OWN, COLS), jnp.bfloat16),
+            pltpu.VMEM((256, R), jnp.bfloat16),
+            pltpu.VMEM((256, COLS), jnp.bfloat16),
+            pltpu.VMEM((2, OWN, COLS), jnp.float32),
         ),
         in_specs=[any_space] * 6,
-        out_specs=[any_space] * 3,
+        out_specs=[vmem] * 4,
         scratch_shapes=[
             pltpu.VMEM((TOK, 256), jnp.bfloat16),
             pltpu.VMEM((256, R), jnp.bfloat16),
-            pltpu.VMEM((256, R), jnp.bfloat16),
             pltpu.VMEM((NX, 512, COLS), jnp.bfloat16),
-            pltpu.VMEM((256, COLS), jnp.bfloat16),
             pltpu.VMEM((NYH, 2, OWN, COLS), jnp.float32),
-            pltpu.VMEM((2, NYH, OWN, COLS), jnp.float32),
-            pltpu.VMEM((256, COLS), jnp.bfloat16),
             pltpu.VMEM((NQ, NYH * OWN, TOK), A_TYPE),
             pltpu.VMEM((NQ, NYH * OWN, TOK), A_TYPE),
             pltpu.VMEM((NY, NYH * OWN, TOK), jnp.float32),
             pltpu.VMEM((NX - 1, NYH * OWN, COLS), D_TYPE),
             pltpu.VMEM((NX - 1, NYH * OWN, COLS), D_TYPE),
-            pltpu.VMEM((NQ, NYH * OWN, COLS), jnp.bfloat16),
             pltpu.VMEM((NYH * OWN, COLS), jnp.float32),
             pltpu.SemaphoreType.DMA((9,)),
-            pltpu.SemaphoreType.DMA((3,)),
             pltpu.SemaphoreType.DMA((2,)),
             pltpu.SemaphoreType.DMA((2, NQ)),
             pltpu.SemaphoreType.DMA((2, NY)),
@@ -223,10 +221,23 @@
             pltpu.SemaphoreType.DMA((2, NZ)),
         ],
         compiler_params=pltpu.CompilerParams(
-            collective_id=0, has_side_effects=True, vmem_limit_bytes=60 * 1024 * 1024
+            collective_id=0, has_side_effects=True, vmem_limit_bytes=56 * 1024 * 1024
         ),
-        name="galore_step",
+        name="directions",
     )(activations, out_grads, projector, weight, moment, second)
+    return pl.pallas_call(
+        finish,
+        out_shape=(
+            jax.ShapeDtypeStruct(weight.shape, jnp.bfloat16),
+            jax.ShapeDtypeStruct(moment.shape, jnp.float32),
+            jax.ShapeDtypeStruct(second.shape, jnp.float32),
+        ),
+        in_specs=[vmem] * 4,
+        out_specs=[any_space] * 3,
+        scratch_shapes=[pltpu.VMEM((256, COLS), jnp.bfloat16), pltpu.SemaphoreType.DMA((3,))],
+        compiler_params=pltpu.CompilerParams(vmem_limit_bytes=4 * 1024 * 1024),
+        name="finish",
+    )(*held)
 
 
 def solution(mesh):

time: 47.3 us -> 42.7 us (0.903)
  local copies, waits for them, and re-layouts: 4.54 us -> 0 us
    unnamed x3 -> x0, local copies, waits for them, and re-layouts: 4.54 us -> none
    pallas_call x1 -> x2, Pallas kernels: 41.8 us -> 41.9 us  [the longest x1 40.8 us: per_device(): pl.pallas_call(kernel, out_shape=(pltpu.VMEM((NQ, NYH * OWN, COLS), jnp.b...]
where the time goes in v2:
time: 42.7 us; the launch traced here: 42.5 us
  Pallas kernels  41.9 us (98%)
  between operations  0.64 us (1%)
    pallas_call x1, Pallas kernels, per_device(): pl.pallas_call(kernel, out_shape=(pltpu.VMEM((NQ, NYH * OWN, COLS), jnp.b...  40.8 us
    pallas_call x1, Pallas kernels, per_device(): pl.pallas_call(finish, out_shape=(jax.ShapeDtypeStruct(weight.shape, jnp....  1.1 us

profile of v2, /device:TPU:1, one launch (start us, length us, event | category | flops | bytes accessed | tf_op | source)
XLA Modules:
  0.0 42.5 jit_solution(311417551406046454)
XLA Ops:
  0.6 40.8 %directions.1 = (bf16[16,16,896]{2,1,0:T(8,128)(2,1)S(1)}, bf16[256,256]{1,0:T(8,128)(2,1)S(1)}, bf16[256,896]{1,0:T(8,128)(2,1)S(1)}, f32[2,8,896]{2,1,0:T(8,128)S(1)}) custom-call(bf16[512,256]{1,0:T(8,128)(2,1)} %act.1, bf16[512,3584]{1,0:T(8,128)(2,1)} %grads.1, bf16[256,256]{1,0:T(8,128)(2,1)} %proj.1, bf16[256,896]{1,0:T(8,128)(2,1)} %weight.1, ...), custom_call_target="tpu_custom_call" | custom-call | tf_op jit(solution)/shard_map/directions/pallas_call | solution.py:194
  41.4 1.1 %finish.1 = (bf16[256,896]{1,0:T(8,128)(2,1)}, f32[8,896]{1,0:T(8,128)}, f32[8,896]{1,0:T(8,128)}) custom-call(bf16[16,16,896]{2,1,0:T(8,128)(2,1)S(1)} %get-tuple-element.7.dirs, bf16[256,256]{1,0:T(8,128)(2,1)S(1)} %get-tuple-element.8.perm, bf16[256,896]{1,0:T(8,128)(2,1)S(1)} %get-tuple-element.9.weight, f32[2,8,896]{2,1,0:T(8,128)S(1)} %get-tuple-element.10.state), custom_call_target="tpu_custom_call" | custom-call | tf_op jit(solution)/shard_map/finish/pallas_call | solution.py:228

commit v3 on v2

v3 whole, which is shorter than its diff:
```python
import jax
import jax.numpy as jnp
from jax import lax
from jax.experimental import pallas as pl
from jax.experimental.pallas import tpu as pltpu
from jax.sharding import PartitionSpec as P

MESH = pl.DeviceIdType.MESH
A_TYPE = jnp.bfloat16
NEAR = (0, 1, 7)
D_TYPE = jnp.float32

NZ, NK, NYH, NYL, NX = 8, 2, 2, 4, 4
NQ, NY = NZ * NK, NYH * NYL
OWN = 8
TOK = 128
R = 256
COLS = 896
CHUNKS = (pl.ds(0, 512), pl.ds(512, 384))
FAR_FIRST = (4, 3, 5, 2, 6, 1, 7)
NEAR_FIRST = (1, 7, 2, 6, 3, 5, 4)
F_ORDER = FAR_FIRST
PASSED_ON = ((1, 2), (3, 2), (5, 2), (7, 1))
FIRST_FIX = 1.0 / (1.0 - 0.9**10)
SECOND_FIX = 1.0 / (1.0 - 0.999**10)


def kernel(
    act, grads, proj, weight, moment, second,
    out_v, state_v,
    act_v, proj_v, perm_v, weight_v, grads_v, mv, near_a, far_a, got_near_a, got_far_a, recv_b, send_d, recv_d, low_v, dirs,
    in_sem, mv_sem, a_sem, b_sem, d_sem, f_send, f_recv, c_send, c_recv,
):
    row, col, dp = lax.axis_index("row"), lax.axis_index("col"), lax.axis_index("dp")
    yh, z, k = row // NQ, (row // NK) % NZ, row % NK
    y, q = yh * NYL + col, row % NQ

    def at_zk(dz, dk):
        return (yh * NQ + ((z + dz) % NZ) * NK + (k + dk) % NK, col, dp)

    def at_y(dy):
        to = (y + dy) % NY
        return ((to // NYL) * NQ + q, to % NYL, dp)

    def at_x(dx):
        return (row, col, (dp + dx) % NX)

    zk = [(dz, dk) for dz in FAR_FIRST for dk in range(NK)] + [(0, 1)]

    loads = [
        pltpu.make_async_copy(act.at[pl.ds(pl.multiple_of(col * TOK, TOK), TOK), :], act_v, in_sem.at[0]),
        pltpu.make_async_copy(proj, proj_v, in_sem.at[1]),
        pltpu.make_async_copy(moment, mv.at[yh, 0], in_sem.at[2]),
        pltpu.make_async_copy(second, mv.at[yh, 1], in_sem.at[3]),
    ]
    for x in range(NX):
        loads.append(pltpu.make_async_copy(grads.at[:, pl.ds(x * COLS, COLS)], grads_v.at[x], in_sem.at[4 + x]))
    loads.append(pltpu.make_async_copy(weight, weight_v, in_sem.at[8]))
    barrier = pltpu.get_barrier_semaphore()
    peers = []
    for far in FAR_FIRST:
        peers += [at_zk(far, 1), at_zk(far, 0), at_y(far)] + ([at_x(far)] if far < NX else [])
    peers.append(at_zk(0, 1))
    for peer in peers:
        pl.semaphore_signal(barrier, inc=1, device_id=peer, device_id_type=MESH)
    for load in loads:
        load.start()

    loads[0].wait()
    loads[1].wait()
    part = lax.dot_general(proj_v[...], act_v[...], (((0,), (1,)), ((), ())), preferred_element_type=jnp.float32)
    part = part.reshape(NYH, NQ, OWN, TOK)
    part = jnp.concatenate([part[0], part[1]], axis=1)
    near_a[...] = part
    far_a[...] = part.astype(A_TYPE)

    pl.semaphore_wait(barrier, len(peers))

    sends_a = []
    for j, (dz, dk) in enumerate(zk):
        to = ((z + dz) % NZ) * NK + (k + dk) % NK
        sent, got = (near_a, got_near_a) if dz in NEAR else (far_a, got_far_a)
        copy = pltpu.make_async_remote_copy(
            src_ref=sent.at[to], dst_ref=got.at[j], send_sem=a_sem.at[0, j], recv_sem=a_sem.at[1, j],
            device_id=at_zk(dz, dk), device_id_type=MESH,
        )
        copy.start()
        sends_a.append((copy, got.at[j]))

    loads[2].wait()
    loads[3].wait()
    send_mv = pltpu.make_async_remote_copy(
        src_ref=mv.at[yh], dst_ref=mv.at[yh], send_sem=mv_sem.at[0], recv_sem=mv_sem.at[1],
        device_id=at_y(NYL), device_id_type=MESH,
    )
    send_mv.start()

    source = lax.broadcasted_iota(jnp.int32, (R, R), 0)
    place = lax.broadcasted_iota(jnp.int32, (R, R), 1)
    core, step, half, rank = place // (R // NK), place // (NYH * OWN) % NZ, place // OWN % NYH, place % OWN
    from_z = (z + NZ - jnp.where(step % 2 == 1, (step + 1) // 2, (NZ - step // 2) % NZ)) % NZ
    wanted = ((half * NZ + from_z) * NK + core) * OWN + rank
    shuffle = jnp.where(source == wanted, 1.0, 0.0).astype(jnp.bfloat16)
    perm_v[...] = jnp.dot(proj_v[...], shuffle, preferred_element_type=jnp.float32).astype(jnp.bfloat16)

    total = near_a[q]
    for copy, got in reversed(sends_a):
        copy.wait_recv()
        total += got[...].astype(jnp.float32)
    sends_a = [copy for copy, _ in sends_a]

    recv_b[y] = total
    sends_b = []
    for j, dy in enumerate(FAR_FIRST):
        copy = pltpu.make_async_remote_copy(
            src_ref=recv_b.at[y], dst_ref=recv_b.at[y], send_sem=b_sem.at[0, j], recv_sem=b_sem.at[1, j],
            device_id=at_y(dy), device_id_type=MESH,
        )
        copy.start()
        sends_b.append(copy)
    for load in loads[4:8]:
        load.wait()
    for copy in sends_b:
        copy.wait_recv()
    coords = jnp.concatenate([recv_b[c] + recv_b[NYL + c] for c in range(NYL)], axis=1)
    high = coords.astype(jnp.bfloat16)
    rest = (coords - high.astype(jnp.float32)).astype(jnp.bfloat16)
    both = jnp.concatenate([high, rest], axis=0)

    def low_of(to, at):
        product = jnp.dot(both, grads_v[to, :, at], preferred_element_type=jnp.float32)
        return product[: NYH * OWN] + product[NYH * OWN :]

    sends_d = []
    for c, at in enumerate(CHUNKS):
        for j, dx in enumerate((2, 1, 3)):
            send_d[j, :, at] = low_of((dp + dx) % NX, at).astype(D_TYPE)
            copy = pltpu.make_async_remote_copy(
                src_ref=send_d.at[j, :, at], dst_ref=recv_d.at[j, :, at],
                send_sem=d_sem.at[0, c, j], recv_sem=d_sem.at[1, c, j],
                device_id=at_x(dx), device_id_type=MESH,
            )
            copy.start()
            sends_d.append(copy)
    for at in CHUNKS:
        low_v[:, at] = low_of(dp, at)
    send_mv.wait_recv()

    def passed(to, source, target, send_sem, recv_sem):
        return pltpu.make_async_remote_copy(
            src_ref=source, dst_ref=target, send_sem=send_sem, recv_sem=recv_sem, device_id=to, device_id_type=MESH
        )

    def over_z(dz, j, c, at):
        return passed(
            at_zk(dz, 1 - k), dirs.at[k, 0, :, at], dirs.at[k, 1 + j, :, at], f_send.at[c, j], f_recv.at[c, j, k]
        )

    def over_core(g, c, at):
        here = dirs.at[:, pl.ds(*PASSED_ON[g]), :, at]
        return passed(at_zk(0, 1), here, here, c_send.at[c, 1 + g], c_recv.at[c, 1 + g])

    sends_f, sends_c = [], []
    for c, at in enumerate(CHUNKS):
        for copy in sends_d[c * (NX - 1) : (c + 1) * (NX - 1)]:
            copy.wait_recv()
        low = low_v[:, at]
        for j in (1, 2, 0):
            low += recv_d[j, :, at].astype(jnp.float32)
        low = (low * (1.0 / NX)).reshape(NYH, OWN, -1)
        state_m = 0.9 * mv[:, 0, :, at] + 0.1 * low
        state_s = 0.999 * mv[:, 1, :, at] + 0.001 * low * low
        direction = state_m * FIRST_FIX / (jnp.sqrt(state_s * SECOND_FIX) + 1e-08)
        dirs[k, 0, :, at] = direction.reshape(NYH * OWN, -1).astype(jnp.bfloat16)
        for dz in F_ORDER:
            sends_f.append(over_z(dz, NEAR_FIRST.index(dz), c, at))
            sends_f[-1].start()
        own = dirs.at[k, 0, :, at]
        sends_c.append(passed(at_zk(0, 1), own, own, c_send.at[c, 0], c_recv.at[c, 0]))
        sends_c[c].start()
        state_v[0, :, at] = jnp.where(yh == 0, state_m[0], state_m[1])
        state_v[1, :, at] = jnp.where(yh == 0, state_s[0], state_s[1])
    loads[8].wait()

    def update(at):
        product = jnp.dot(perm_v[...], dirs[:, :, :, at].reshape(R, -1), preferred_element_type=jnp.float32)
        out_v[:, at] = (weight_v[:, at].astype(jnp.float32) - 0.5 * product).astype(jnp.bfloat16)

    @pl.when(k == 1)
    def _():
        for c, at in enumerate(CHUNKS):
            for g, (first, count) in enumerate(PASSED_ON):
                for j in range(first - 1, first - 1 + count):
                    for core in range(NK):
                        ref = dirs.at[core, 1 + j, :, at]
                        passed(at_zk(0, 1), ref, ref, f_send.at[c, j], f_recv.at[c, j, core]).wait_recv()
                over_core(g, c, at).start()
        for c, at in enumerate(CHUNKS):
            sends_c[c].wait_recv()
            update(at)
        for c, at in enumerate(CHUNKS):
            for g in range(len(PASSED_ON)):
                over_core(g, c, at).wait_send()

    @pl.when(k == 0)
    def _():
        for c, at in enumerate(CHUNKS):
            sends_c[c].wait_recv()
            for g in range(len(PASSED_ON)):
                over_core(g, c, at).wait_recv()
            update(at)

    for copy in sends_a + [send_mv] + sends_b + sends_d + sends_f + sends_c:
        copy.wait_send()


def store(weight, state, new_weight, new_moment, new_second, out_sem):
    copies = [
        pltpu.make_async_copy(weight, new_weight, out_sem.at[0]),
        pltpu.make_async_copy(state.at[0], new_moment, out_sem.at[1]),
        pltpu.make_async_copy(state.at[1], new_second, out_sem.at[2]),
    ]
    for copy in copies:
        copy.start()
    for copy in copies:
        copy.wait()


def per_device(activations, out_grads, projector, weight, moment, second):
    any_space = pl.BlockSpec(memory_space=pl.ANY)
    vmem = pl.BlockSpec(memory_space=pltpu.VMEM)
    held = pl.pallas_call(
        kernel,
        out_shape=(
            pltpu.VMEM((256, COLS), jnp.bfloat16),
            pltpu.VMEM((2, OWN, COLS), jnp.float32),
        ),
        in_specs=[any_space] * 6,
        out_specs=[vmem] * 2,
        scratch_shapes=[
            pltpu.VMEM((TOK, 256), jnp.bfloat16),
            pltpu.VMEM((256, R), jnp.bfloat16),
            pltpu.VMEM((256, R), jnp.bfloat16),
            pltpu.VMEM((256, COLS), jnp.bfloat16),
            pltpu.VMEM((NX, 512, COLS), jnp.bfloat16),
            pltpu.VMEM((NYH, 2, OWN, COLS), jnp.float32),
            pltpu.VMEM((NQ, NYH * OWN, TOK), jnp.float32),
            pltpu.VMEM((NQ, NYH * OWN, TOK), A_TYPE),
            pltpu.VMEM((NQ, NYH * OWN, TOK), jnp.float32),
            pltpu.VMEM((NQ, NYH * OWN, TOK), A_TYPE),
            pltpu.VMEM((NY, NYH * OWN, TOK), jnp.float32),
            pltpu.VMEM((NX - 1, NYH * OWN, COLS), D_TYPE),
            pltpu.VMEM((NX - 1, NYH * OWN, COLS), D_TYPE),
            pltpu.VMEM((NYH * OWN, COLS), jnp.float32),
            pltpu.VMEM((NK, NZ, NYH * OWN, COLS), jnp.bfloat16),
            pltpu.SemaphoreType.DMA((9,)),
            pltpu.SemaphoreType.DMA((2,)),
            pltpu.SemaphoreType.DMA((2, NQ)),
            pltpu.SemaphoreType.DMA((2, NY)),
            pltpu.SemaphoreType.DMA((2, len(CHUNKS), NX)),
            pltpu.SemaphoreType.DMA((len(CHUNKS), NZ)),
            pltpu.SemaphoreType.DMA((len(CHUNKS), NZ, NK)),
            pltpu.SemaphoreType.DMA((len(CHUNKS), NZ)),
            pltpu.SemaphoreType.DMA((len(CHUNKS), NZ)),
        ],
        compiler_params=pltpu.CompilerParams(
            collective_id=0, has_side_effects=True, vmem_limit_bytes=56 * 1024 * 1024
        ),
        name="directions",
    )(activations, out_grads, projector, weight, moment, second)
    return pl.pallas_call(
        store,
        out_shape=(
            jax.ShapeDtypeStruct(weight.shape, jnp.bfloat16),
            jax.ShapeDtypeStruct(moment.shape, jnp.float32),
            jax.ShapeDtypeStruct(second.shape, jnp.float32),
        ),
        in_specs=[vmem] * 2,
        out_specs=[any_space] * 3,
        scratch_shapes=[pltpu.SemaphoreType.DMA((3,))],
        compiler_params=pltpu.CompilerParams(vmem_limit_bytes=4 * 1024 * 1024),
        name="store",
    )(*held)


def solution(mesh):
    in_specs = (
        P("dp", "row"),
        P("dp", "col"),
        P("row", None),
        P("row", ("col", "dp")),
        P("row", ("col", "dp")),
        P("row", ("col", "dp")),
    )
    out_specs = (P("row", ("col", "dp")), P("row", ("col", "dp")), P("row", ("col", "dp")))
    return jax.shard_map(
        per_device, mesh=mesh, in_specs=in_specs, out_specs=out_specs, check_vma=False
    )
```

time: 42.7 us -> 39.7 us (0.930)
  Pallas kernels: 41.9 us -> 39 us
    pallas_call x2, Pallas kernels: 41.9 us -> 39 us  [the longest x1 38.2 us: per_device(): pl.pallas_call(kernel, out_shape=(pltpu.VMEM((256, COLS), jnp.bfloat16),...]
where the time goes in v3:
time: 39.7 us; the launch traced here: 39.6 us
  Pallas kernels  39 us (98%)
  between operations  0.64 us (2%)
    pallas_call x1, Pallas kernels, per_device(): pl.pallas_call(kernel, out_shape=(pltpu.VMEM((256, COLS), jnp.bfloat16),...  38.2 us
    pallas_call x1, Pallas kernels, per_device(): pl.pallas_call(store, out_shape=(jax.ShapeDtypeStruct(weight.shape, jnp.b...  0.8 us

profile of v3, /device:TPU:1, one launch (start us, length us, event | category | flops | bytes accessed | tf_op | source)
XLA Modules:
  0.0 39.6 jit_solution(14127383351172545527)
XLA Ops:
  0.6 38.2 %directions.1 = (bf16[256,896]{1,0:T(8,128)(2,1)S(1)}, f32[2,8,896]{2,1,0:T(8,128)S(1)}) custom-call(bf16[512,256]{1,0:T(8,128)(2,1)} %act.1, bf16[512,3584]{1,0:T(8,128)(2,1)} %grads.1, bf16[256,256]{1,0:T(8,128)(2,1)} %proj.1, bf16[256,896]{1,0:T(8,128)(2,1)} %weight.1, f32[8,896]{1,0:T(8,128)} %moment.1, f32[8,896]{1,0:T(8,128)} %second.1), custom_call_target="tpu_custom_call" | custom-call | tf_op jit(solution)/shard_map/directions/pallas_call | solution.py:232
  38.8 0.8 %store.1 = (bf16[256,896]{1,0:T(8,128)(2,1)}, f32[8,896]{1,0:T(8,128)}, f32[8,896]{1,0:T(8,128)}) custom-call(bf16[256,896]{1,0:T(8,128)(2,1)S(1)} %get-tuple-element.5.weight, f32[2,8,896]{2,1,0:T(8,128)S(1)} %get-tuple-element.6.state), custom_call_target="tpu_custom_call" | custom-call | tf_op jit(solution)/shard_map/store/pallas_call | solution.py:271

commit v4 on v3

v4 whole, which is shorter than its diff:
```python
import jax
import jax.numpy as jnp
from jax import lax
from jax.experimental import pallas as pl
from jax.experimental.pallas import tpu as pltpu
from jax.sharding import PartitionSpec as P

MESH = pl.DeviceIdType.MESH
NZ, NK, NYH, NYL, NX = 8, 2, 2, 4, 4
NQ, NY = NZ * NK, NYH * NYL
OWN = 8
TOK = 128
R = 256
COLS = 896
CHUNKS = (pl.ds(0, 512), pl.ds(512, 384))
FAR_FIRST = (4, 3, 5, 2, 6, 1, 7)
FAR, NEAR = FAR_FIRST[:5], FAR_FIRST[5:]
GROUPS = ((1, 1), (2, 2), (4, 2), (6, 2))
FIRST_FIX = 1.0 / (1.0 - 0.9**10)
SECOND_FIX = 1.0 / (1.0 - 0.999**10)


def kernel(
    act, grads, proj, weight, moment, second,
    out_v, state_v,
    first_v, perm_v, weight_v, grads_v, mv, near_a, far_a, got_near_a, got_far_a, recv_b, send_d, recv_d, low_v, dirs,
    first_sem, mv_in_sem, grads_sem, weight_sem, mv_sem, near_sem, far_sem, b_sem, d_send, d_recv, f_send, f_recv,
    own_send, own_recv, pass_send, pass_recv,
):
    row, col, dp = lax.axis_index("row"), lax.axis_index("col"), lax.axis_index("dp")
    yh, z, k = row // NQ, (row // NK) % NZ, row % NK
    y, q = yh * NYL + col, row % NQ

    def at_zk(dz, dk):
        return (yh * NQ + ((z + dz) % NZ) * NK + (k + dk) % NK, col, dp)

    def at_y(dy):
        to = (y + dy) % NY
        return ((to // NYL) * NQ + q, to % NYL, dp)

    def at_x(dx):
        return (row, col, (dp + dx) % NX)

    def send(source, target, send_sem, recv_sem, to):
        copy = pltpu.make_async_remote_copy(
            src_ref=source, dst_ref=target, send_sem=send_sem, recv_sem=recv_sem, device_id=to, device_id_type=MESH
        )
        copy.start()

    def wait(ref, sem):
        pltpu.make_async_copy(ref, ref, sem).wait()

    barrier = pltpu.get_barrier_semaphore()
    peers = []
    for far in FAR_FIRST:
        peers += [at_zk(far, 1), at_zk(far, 0), at_y(far)] + ([at_x(far)] if far < NX else [])
    peers.append(at_zk(0, 1))
    for peer in peers:
        pl.semaphore_signal(barrier, inc=1, device_id=peer, device_id_type=MESH)

    tokens = pl.ds(pl.multiple_of(col * TOK, TOK), TOK)
    pltpu.make_async_copy(act.at[tokens, :], first_v.at[pl.ds(0, TOK), :], first_sem).start()
    pltpu.make_async_copy(proj, first_v.at[pl.ds(TOK, R), :], first_sem).start()
    pltpu.make_async_copy(moment, mv.at[yh, 0], mv_in_sem).start()
    pltpu.make_async_copy(second, mv.at[yh, 1], mv_in_sem).start()
    for x in range(NX):
        pltpu.make_async_copy(grads.at[:, pl.ds(x * COLS, COLS)], grads_v.at[x], grads_sem).start()
    pltpu.make_async_copy(weight, weight_v, weight_sem).start()

    wait(first_v, first_sem)
    block = first_v[TOK:]
    part = lax.dot_general(block, first_v[:TOK], (((0,), (1,)), ((), ())), preferred_element_type=jnp.float32)
    part = part.reshape(NYH, NQ, OWN, TOK)
    part = jnp.concatenate([part[0], part[1]], axis=1)
    near_a[...] = part
    far_a[...] = part.astype(jnp.bfloat16)

    pl.semaphore_wait(barrier, len(peers))

    for i, (dz, dk) in enumerate([(dz, dk) for dz in FAR for dk in range(NK)]):
        to = ((z + dz) % NZ) * NK + (k + dk) % NK
        send(far_a.at[to], got_far_a.at[i], far_sem.at[0], far_sem.at[1], at_zk(dz, dk))
    for i, (dz, dk) in enumerate([(dz, dk) for dz in NEAR for dk in range(NK)] + [(0, 1)]):
        to = ((z + dz) % NZ) * NK + (k + dk) % NK
        send(near_a.at[to], got_near_a.at[i], near_sem.at[0], near_sem.at[1], at_zk(dz, dk))

    source = lax.broadcasted_iota(jnp.int32, (R, R), 0)
    place = lax.broadcasted_iota(jnp.int32, (R, R), 1)
    step, core, half, rank = place // (R // NZ), place // (NYH * OWN) % NK, place // OWN % NYH, place % OWN
    from_z = (z + NZ - jnp.where(step % 2 == 1, (step + 1) // 2, (NZ - step // 2) % NZ)) % NZ
    wanted = ((half * NZ + from_z) * NK + core) * OWN + rank
    shuffle = jnp.where(source == wanted, 1.0, 0.0).astype(jnp.bfloat16)
    perm_v[...] = jnp.dot(block, shuffle, preferred_element_type=jnp.float32).astype(jnp.bfloat16)

    wait(got_near_a, near_sem.at[1])
    total = near_a[q] + jnp.sum(got_near_a[...], axis=0)
    wait(got_far_a, far_sem.at[1])
    total += jnp.sum(got_far_a[...].astype(jnp.float32), axis=0)

    recv_b[y] = total
    for dy in FAR_FIRST:
        send(recv_b.at[y], recv_b.at[y], b_sem.at[0], b_sem.at[1], at_y(dy))

    wait(mv.at[yh], mv_in_sem)
    send(mv.at[yh], mv.at[yh], mv_sem.at[0], mv_sem.at[1], at_y(NYL))

    wait(grads_v, grads_sem)
    wait(recv_b.at[pl.ds(0, NY - 1)], b_sem.at[1])
    coords = jnp.concatenate([recv_b[c] + recv_b[NYL + c] for c in range(NYL)], axis=1)
    high = coords.astype(jnp.bfloat16)
    rest = (coords - high.astype(jnp.float32)).astype(jnp.bfloat16)
    both = jnp.concatenate([high, rest], axis=0)

    def low_of(to, at):
        product = jnp.dot(both, grads_v[to, :, at], preferred_element_type=jnp.float32)
        return product[: NYH * OWN] + product[NYH * OWN :]

    for c, at in enumerate(CHUNKS):
        for j, dx in enumerate((2, 1, 3)):
            send_d[j, :, at] = low_of((dp + dx) % NX, at)
            send(send_d.at[j, :, at], recv_d.at[j, :, at], d_send, d_recv.at[c], at_x(dx))
    for at in CHUNKS:
        low_v[:, at] = low_of(dp, at)
    wait(mv.at[yh], mv_sem.at[1])

    for c, at in enumerate(CHUNKS):
        wait(recv_d.at[:, :, at], d_recv.at[c])
        low = low_v[:, at] + recv_d[1, :, at] + recv_d[2, :, at] + recv_d[0, :, at]
        low = (low * (1.0 / NX)).reshape(NYH, OWN, -1)
        state_m = 0.9 * mv[:, 0, :, at] + 0.1 * low
        state_s = 0.999 * mv[:, 1, :, at] + 0.001 * low * low
        direction = state_m * FIRST_FIX / (jnp.sqrt(state_s * SECOND_FIX) + 1e-08)
        dirs[0, k, :, at] = direction.reshape(NYH * OWN, -1).astype(jnp.bfloat16)
        own = dirs.at[0, k, :, at]
        for i in range(NZ - 1):
            dz = (i + (i - z + NZ) // NZ - z + NZ) % NZ
            back = dz // (NZ // 2 + 1)
            slot = (2 * dz - 1) * (1 - back) + (2 * NZ - 2 * dz) * back
            send(own, dirs.at[slot, k, :, at], f_send, f_recv.at[c, slot // 2], at_zk(dz, 1 - k))
        send(own, own, own_send, own_recv.at[c], at_zk(0, 1))
        state_v[0, :, at] = jnp.where(yh == 0, state_m[0], state_m[1])
        state_v[1, :, at] = jnp.where(yh == 0, state_s[0], state_s[1])
    wait(weight_v, weight_sem)

    def update(at):
        product = jnp.dot(perm_v[...], dirs[:, :, :, at].reshape(R, -1), preferred_element_type=jnp.float32)
        out_v[:, at] = (weight_v[:, at].astype(jnp.float32) - 0.5 * product).astype(jnp.bfloat16)

    @pl.when(k == 1)
    def _():
        for c, at in enumerate(CHUNKS):
            for g, (first, count) in enumerate(GROUPS):
                here = dirs.at[pl.ds(first, count), :, :, at]
                wait(here, f_recv.at[c, g])
                send(here, here, pass_send, pass_recv.at[c], at_zk(0, 1))
        for c, at in enumerate(CHUNKS):
            wait(dirs.at[0, 0, :, at], own_recv.at[c])
            update(at)
        wait(dirs.at[pl.ds(1, NZ - 1)], pass_send)

    @pl.when(k == 0)
    def _():
        for c, at in enumerate(CHUNKS):
            wait(dirs.at[0, 0, :, at], own_recv.at[c])
            wait(dirs.at[pl.ds(1, NZ - 1), :, :, at], pass_recv.at[c])
            update(at)

    wait(far_a.at[pl.ds(0, len(FAR) * NK)], far_sem.at[0])
    wait(near_a.at[pl.ds(0, len(NEAR) * NK + 1)], near_sem.at[0])
    wait(mv.at[0], mv_sem.at[0])
    wait(recv_b.at[pl.ds(0, NY - 1)], b_sem.at[0])
    wait(send_d, d_send)
    wait(dirs.at[pl.ds(0, NZ - 1), 0], f_send)
    wait(dirs.at[0, 0], own_send)


def store(weight, state, new_weight, new_moment, new_second, out_sem):
    copies = [
        pltpu.make_async_copy(weight, new_weight, out_sem.at[0]),
        pltpu.make_async_copy(state.at[0], new_moment, out_sem.at[1]),
        pltpu.make_async_copy(state.at[1], new_second, out_sem.at[2]),
    ]
    for copy in copies:
        copy.start()
    for copy in copies:
        copy.wait()


def per_device(activations, out_grads, projector, weight, moment, second):
    any_space = pl.BlockSpec(memory_space=pl.ANY)
    vmem = pl.BlockSpec(memory_space=pltpu.VMEM)
    held = pl.pallas_call(
        kernel,
        out_shape=(
            pltpu.VMEM((256, COLS), jnp.bfloat16),
            pltpu.VMEM((2, OWN, COLS), jnp.float32),
        ),
        in_specs=[any_space] * 6,
        out_specs=[vmem] * 2,
        scratch_shapes=[
            pltpu.VMEM((TOK + R, R), jnp.bfloat16),
            pltpu.VMEM((256, R), jnp.bfloat16),
            pltpu.VMEM((256, COLS), jnp.bfloat16),
            pltpu.VMEM((NX, 512, COLS), jnp.bfloat16),
            pltpu.VMEM((NYH, 2, OWN, COLS), jnp.float32),
            pltpu.VMEM((NQ, NYH * OWN, TOK), jnp.float32),
            pltpu.VMEM((NQ, NYH * OWN, TOK), jnp.bfloat16),
            pltpu.VMEM((len(NEAR) * NK + 1, NYH * OWN, TOK), jnp.float32),
            pltpu.VMEM((len(FAR) * NK, NYH * OWN, TOK), jnp.bfloat16),
            pltpu.VMEM((NY, NYH * OWN, TOK), jnp.float32),
            pltpu.VMEM((NX - 1, NYH * OWN, COLS), jnp.float32),
            pltpu.VMEM((NX - 1, NYH * OWN, COLS), jnp.float32),
            pltpu.VMEM((NYH * OWN, COLS), jnp.float32),
            pltpu.VMEM((NZ, NK, NYH * OWN, COLS), jnp.bfloat16),
            *[pltpu.SemaphoreType.DMA(())] * 4,
            *[pltpu.SemaphoreType.DMA((2,))] * 4,
            pltpu.SemaphoreType.DMA(()),
            pltpu.SemaphoreType.DMA((len(CHUNKS),)),
            pltpu.SemaphoreType.DMA(()),
            pltpu.SemaphoreType.DMA((len(CHUNKS), len(GROUPS))),
            pltpu.SemaphoreType.DMA(()),
            pltpu.SemaphoreType.DMA((len(CHUNKS),)),
            pltpu.SemaphoreType.DMA(()),
            pltpu.SemaphoreType.DMA((len(CHUNKS),)),
        ],
        compiler_params=pltpu.CompilerParams(
            collective_id=0, has_side_effects=True, vmem_limit_bytes=56 * 1024 * 1024
        ),
        name="directions",
    )(activations, out_grads, projector, weight, moment, second)
    return pl.pallas_call(
        store,
        out_shape=(
            jax.ShapeDtypeStruct(weight.shape, jnp.bfloat16),
            jax.ShapeDtypeStruct(moment.shape, jnp.float32),
            jax.ShapeDtypeStruct(second.shape, jnp.float32),
        ),
        in_specs=[vmem] * 2,
        out_specs=[any_space] * 3,
        scratch_shapes=[pltpu.SemaphoreType.DMA((3,))],
        compiler_params=pltpu.CompilerParams(vmem_limit_bytes=4 * 1024 * 1024),
        name="store",
    )(*held)


def solution(mesh):
    in_specs = (
        P("dp", "row"),
        P("dp", "col"),
        P("row", None),
        P("row", ("col", "dp")),
        P("row", ("col", "dp")),
        P("row", ("col", "dp")),
    )
    out_specs = (P("row", ("col", "dp")), P("row", ("col", "dp")), P("row", ("col", "dp")))
    return jax.shard_map(
        per_device, mesh=mesh, in_specs=in_specs, out_specs=out_specs, check_vma=False
    )
```

time: 39.7 us -> 38.1 us (0.960)
  Pallas kernels: 39 us -> 37.3 us
    pallas_call x1, Pallas kernels: 38.2 us -> 36.5 us  [per_device(): pl.pallas_call(kernel, out_shape=(pltpu.VMEM((256, COLS), jnp.bfloat16),...]
where the time goes in v4:
time: 38.1 us; the launch traced here: 38 us
  Pallas kernels  37.3 us (98%)
  between operations  0.64 us (2%)
    pallas_call x1, Pallas kernels, per_device(): pl.pallas_call(kernel, out_shape=(pltpu.VMEM((256, COLS), jnp.bfloat16),...  36.5 us
    pallas_call x1, Pallas kernels, per_device(): pl.pallas_call(store, out_shape=(jax.ShapeDtypeStruct(weight.shape, jnp.b...  0.8 us

profile of v4, /device:TPU:1, one launch (start us, length us, event | category | flops | bytes accessed | tf_op | source)
XLA Modules:
  0.0 38.0 jit_solution(2021757152477417221)
XLA Ops:
  0.6 36.5 %directions.1 = (bf16[256,896]{1,0:T(8,128)(2,1)S(1)}, f32[2,8,896]{2,1,0:T(8,128)S(1)}) custom-call(bf16[512,256]{1,0:T(8,128)(2,1)} %act.1, bf16[512,3584]{1,0:T(8,128)(2,1)} %grads.1, bf16[256,256]{1,0:T(8,128)(2,1)} %proj.1, bf16[256,896]{1,0:T(8,128)(2,1)} %weight.1, f32[8,896]{1,0:T(8,128)} %moment.1, f32[8,896]{1,0:T(8,128)} %second.1), custom_call_target="tpu_custom_call" | custom-call | tf_op jit(solution)/shard_map/directions/pallas_call | solution.py:192
  37.2 0.8 %store.1 = (bf16[256,896]{1,0:T(8,128)(2,1)}, f32[8,896]{1,0:T(8,128)}, f32[8,896]{1,0:T(8,128)}) custom-call(bf16[256,896]{1,0:T(8,128)(2,1)S(1)} %get-tuple-element.5.weight, f32[2,8,896]{2,1,0:T(8,128)S(1)} %get-tuple-element.6.state), custom_call_target="tpu_custom_call" | custom-call | tf_op jit(solution)/shard_map/store/pallas_call | solution.py:231

commit v5 on v4

--- a/solution.py
+++ b/solution.py
@@ -15,9 +15,14 @@
 CHUNKS = (pl.ds(0, 512), pl.ds(512, 384))
 FAR_FIRST = (4, 3, 5, 2, 6, 1, 7)
 FAR, NEAR = FAR_FIRST[:5], FAR_FIRST[5:]
+EARLY = 2
 GROUPS = ((1, 1), (2, 2), (4, 2), (6, 2))
 FIRST_FIX = 1.0 / (1.0 - 0.9**10)
 SECOND_FIX = 1.0 / (1.0 - 0.999**10)
+
+
+def other(i, me, n):
+    return (i + (i - me + n) // n - me + n) % n
 
 
 def kernel(
@@ -98,7 +103,7 @@
     total += jnp.sum(got_far_a[...].astype(jnp.float32), axis=0)
 
     recv_b[y] = total
-    for dy in FAR_FIRST:
+    for dy in [other(i, y, NY) for i in range(NY - 1)]:
         send(recv_b.at[y], recv_b.at[y], b_sem.at[0], b_sem.at[1], at_y(dy))
 
     wait(mv.at[yh], mv_in_sem)
@@ -116,30 +121,37 @@
         return product[: NYH * OWN] + product[NYH * OWN :]
 
     for c, at in enumerate(CHUNKS):
-        for j, dx in enumerate((2, 1, 3)):
+        for j in range(NX - 1):
+            dx = other(j, dp, NX)
             send_d[j, :, at] = low_of((dp + dx) % NX, at)
-            send(send_d.at[j, :, at], recv_d.at[j, :, at], d_send, d_recv.at[c], at_x(dx))
+            send(send_d.at[j, :, at], recv_d.at[dx - 1, :, at], d_send, d_recv.at[c], at_x(dx))
     for at in CHUNKS:
         low_v[:, at] = low_of(dp, at)
     wait(mv.at[yh], mv_sem.at[1])
 
+    def over_z(c, at, i):
+        dz = other(i, z, NZ)
+        back = dz // (NZ // 2 + 1)
+        slot = (2 * dz - 1) * (1 - back) + (2 * NZ - 2 * dz) * back
+        send(dirs.at[0, k, :, at], dirs.at[slot, k, :, at], f_send, f_recv.at[c, slot // 2], at_zk(dz, 1 - k))
+
     for c, at in enumerate(CHUNKS):
         wait(recv_d.at[:, :, at], d_recv.at[c])
-        low = low_v[:, at] + recv_d[1, :, at] + recv_d[2, :, at] + recv_d[0, :, at]
+        low = low_v[:, at] + recv_d[0, :, at] + recv_d[1, :, at] + recv_d[2, :, at]
         low = (low * (1.0 / NX)).reshape(NYH, OWN, -1)
         state_m = 0.9 * mv[:, 0, :, at] + 0.1 * low
         state_s = 0.999 * mv[:, 1, :, at] + 0.001 * low * low
         direction = state_m * FIRST_FIX / (jnp.sqrt(state_s * SECOND_FIX) + 1e-08)
         dirs[0, k, :, at] = direction.reshape(NYH * OWN, -1).astype(jnp.bfloat16)
+        for i in range(EARLY):
+            over_z(c, at, i)
         own = dirs.at[0, k, :, at]
-        for i in range(NZ - 1):
-            dz = (i + (i - z + NZ) // NZ - z + NZ) % NZ
-            back = dz // (NZ // 2 + 1)
-            slot = (2 * dz - 1) * (1 - back) + (2 * NZ - 2 * dz) * back
-            send(own, dirs.at[slot, k, :, at], f_send, f_recv.at[c, slot // 2], at_zk(dz, 1 - k))
         send(own, own, own_send, own_recv.at[c], at_zk(0, 1))
         state_v[0, :, at] = jnp.where(yh == 0, state_m[0], state_m[1])
         state_v[1, :, at] = jnp.where(yh == 0, state_s[0], state_s[1])
+    for c, at in enumerate(CHUNKS):
+        for i in range(EARLY, NZ - 1):
+            over_z(c, at, i)
     wait(weight_v, weight_sem)
 
     def update(at):
@@ -153,7 +165,6 @@
                 here = dirs.at[pl.ds(first, count), :, :, at]
                 wait(here, f_recv.at[c, g])
                 send(here, here, pass_send, pass_recv.at[c], at_zk(0, 1))
-        for c, at in enumerate(CHUNKS):
             wait(dirs.at[0, 0, :, at], own_recv.at[c])
             update(at)
         wait(dirs.at[pl.ds(1, NZ - 1)], pass_send)

time: 38.1 us -> 37.3 us (0.979)
  Pallas kernels: 37.3 us -> 36.6 us
    pallas_call x1, Pallas kernels: 36.5 us -> 35.8 us  [per_device(): pl.pallas_call(kernel, out_shape=(pltpu.VMEM((256, COLS), jnp.bfloat16),...]
where the time goes in v5:
time: 37.3 us; the launch traced here: 37.2 us
  Pallas kernels  36.6 us (98%)
  between operations  0.64 us (2%)
    pallas_call x1, Pallas kernels, per_device(): pl.pallas_call(kernel, out_shape=(pltpu.VMEM((256, COLS), jnp.bfloat16),...  35.8 us
    pallas_call x1, Pallas kernels, per_device(): pl.pallas_call(store, out_shape=(jax.ShapeDtypeStruct(weight.shape, jnp.b...  0.8 us

profile of v5, /device:TPU:1, one launch (start us, length us, event | category | flops | bytes accessed | tf_op | source)
XLA Modules:
  0.0 37.2 jit_solution(14594029091723123805)
XLA Ops:
  0.6 35.8 %directions.1 = (bf16[256,896]{1,0:T(8,128)(2,1)S(1)}, f32[2,8,896]{2,1,0:T(8,128)S(1)}) custom-call(bf16[512,256]{1,0:T(8,128)(2,1)} %act.1, bf16[512,3584]{1,0:T(8,128)(2,1)} %grads.1, bf16[256,256]{1,0:T(8,128)(2,1)} %proj.1, bf16[256,896]{1,0:T(8,128)(2,1)} %weight.1, f32[8,896]{1,0:T(8,128)} %moment.1, f32[8,896]{1,0:T(8,128)} %second.1), custom_call_target="tpu_custom_call" | custom-call | tf_op jit(solution)/shard_map/directions/pallas_call | solution.py:203
  36.4 0.8 %store.1 = (bf16[256,896]{1,0:T(8,128)(2,1)}, f32[8,896]{1,0:T(8,128)}, f32[8,896]{1,0:T(8,128)}) custom-call(bf16[256,896]{1,0:T(8,128)(2,1)S(1)} %get-tuple-element.5.weight, f32[2,8,896]{2,1,0:T(8,128)S(1)} %get-tuple-element.6.state), custom_call_target="tpu_custom_call" | custom-call | tf_op jit(solution)/shard_map/store/pallas_call | solution.py:242

commit v6 on v5

--- a/solution.py
+++ b/solution.py
@@ -143,10 +143,10 @@
         state_s = 0.999 * mv[:, 1, :, at] + 0.001 * low * low
         direction = state_m * FIRST_FIX / (jnp.sqrt(state_s * SECOND_FIX) + 1e-08)
         dirs[0, k, :, at] = direction.reshape(NYH * OWN, -1).astype(jnp.bfloat16)
+        own = dirs.at[0, k, :, at]
+        send(own, own, own_send, own_recv.at[c], at_zk(0, 1))
         for i in range(EARLY):
             over_z(c, at, i)
-        own = dirs.at[0, k, :, at]
-        send(own, own, own_send, own_recv.at[c], at_zk(0, 1))
         state_v[0, :, at] = jnp.where(yh == 0, state_m[0], state_m[1])
         state_v[1, :, at] = jnp.where(yh == 0, state_s[0], state_s[1])
     for c, at in enumerate(CHUNKS):

time: 37.3 us -> 37.3 us (level)
  no operation moved by 1% of the time
where the time goes in v6:
time: 37.3 us; the launch traced here: 37.2 us
  Pallas kernels  36.6 us (98%)
  between operations  0.64 us (2%)
    pallas_call x1, Pallas kernels, per_device(): pl.pallas_call(kernel, out_shape=(pltpu.VMEM((256, COLS), jnp.bfloat16),...  35.8 us
    pallas_call x1, Pallas kernels, per_device(): pl.pallas_call(store, out_shape=(jax.ShapeDtypeStruct(weight.shape, jnp.b...  0.8 us

profile of v6, /device:TPU:1, one launch (start us, length us, event | category | flops | bytes accessed | tf_op | source)
XLA Modules:
  0.0 37.2 jit_solution(2059262906884492014)
XLA Ops:
  0.6 35.8 %directions.1 = (bf16[256,896]{1,0:T(8,128)(2,1)S(1)}, f32[2,8,896]{2,1,0:T(8,128)S(1)}) custom-call(bf16[512,256]{1,0:T(8,128)(2,1)} %act.1, bf16[512,3584]{1,0:T(8,128)(2,1)} %grads.1, bf16[256,256]{1,0:T(8,128)(2,1)} %proj.1, bf16[256,896]{1,0:T(8,128)(2,1)} %weight.1, f32[8,896]{1,0:T(8,128)} %moment.1, f32[8,896]{1,0:T(8,128)} %second.1), custom_call_target="tpu_custom_call" | custom-call | tf_op jit(solution)/shard_map/directions/pallas_call | solution.py:203
  36.4 0.8 %store.1 = (bf16[256,896]{1,0:T(8,128)(2,1)}, f32[8,896]{1,0:T(8,128)}, f32[8,896]{1,0:T(8,128)}) custom-call(bf16[256,896]{1,0:T(8,128)(2,1)S(1)} %get-tuple-element.5.weight, f32[2,8,896]{2,1,0:T(8,128)S(1)} %get-tuple-element.6.state), custom_call_target="tpu_custom_call" | custom-call | tf_op jit(solution)/shard_map/store/pallas_call | solution.py:242

commit v7 on v6

--- a/solution.py
+++ b/solution.py
@@ -16,7 +16,7 @@
 FAR_FIRST = (4, 3, 5, 2, 6, 1, 7)
 FAR, NEAR = FAR_FIRST[:5], FAR_FIRST[5:]
 EARLY = 2
-GROUPS = ((1, 1), (2, 2), (4, 2), (6, 2))
+GROUPS = ((1, 3), (4, 4))
 FIRST_FIX = 1.0 / (1.0 - 0.9**10)
 SECOND_FIX = 1.0 / (1.0 - 0.999**10)
 
@@ -133,8 +133,9 @@
         dz = other(i, z, NZ)
         back = dz // (NZ // 2 + 1)
         slot = (2 * dz - 1) * (1 - back) + (2 * NZ - 2 * dz) * back
-        send(dirs.at[0, k, :, at], dirs.at[slot, k, :, at], f_send, f_recv.at[c, slot // 2], at_zk(dz, 1 - k))
-
+        send(dirs.at[0, k, :, at], dirs.at[slot, k, :, at], f_send, f_recv.at[c, slot // 4], at_zk(dz, 1 - k))
+
+    states = []
     for c, at in enumerate(CHUNKS):
         wait(recv_d.at[:, :, at], d_recv.at[c])
         low = low_v[:, at] + recv_d[0, :, at] + recv_d[1, :, at] + recv_d[2, :, at]
@@ -147,11 +148,13 @@
         send(own, own, own_send, own_recv.at[c], at_zk(0, 1))
         for i in range(EARLY):
             over_z(c, at, i)
-        state_v[0, :, at] = jnp.where(yh == 0, state_m[0], state_m[1])
-        state_v[1, :, at] = jnp.where(yh == 0, state_s[0], state_s[1])
+        states.append((state_m, state_s))
     for c, at in enumerate(CHUNKS):
         for i in range(EARLY, NZ - 1):
             over_z(c, at, i)
+    for at, (state_m, state_s) in zip(CHUNKS, states, strict=True):
+        state_v[0, :, at] = jnp.where(yh == 0, state_m[0], state_m[1])
+        state_v[1, :, at] = jnp.where(yh == 0, state_s[0], state_s[1])
     wait(weight_v, weight_sem)
 
     def update(at):

time: 37.3 us -> 37.4 us (level)
  no operation moved by 1% of the time
where the time goes in v7:
time: 37.4 us; the launch traced here: 37.3 us
  Pallas kernels  36.6 us (98%)
  between operations  0.64 us (2%)
    pallas_call x1, Pallas kernels, per_device(): pl.pallas_call(kernel, out_shape=(pltpu.VMEM((256, COLS), jnp.bfloat16),...  35.8 us
    pallas_call x1, Pallas kernels, per_device(): pl.pallas_call(store, out_shape=(jax.ShapeDtypeStruct(weight.shape, jnp.b...  0.8 us

profile of v7, /device:TPU:1, one launch (start us, length us, event | category | flops | bytes accessed | tf_op | source)
XLA Modules:
  0.0 37.3 jit_solution(342352859968167558)
XLA Ops:
  0.6 35.8 %directions.1 = (bf16[256,896]{1,0:T(8,128)(2,1)S(1)}, f32[2,8,896]{2,1,0:T(8,128)S(1)}) custom-call(bf16[512,256]{1,0:T(8,128)(2,1)} %act.1, bf16[512,3584]{1,0:T(8,128)(2,1)} %grads.1, bf16[256,256]{1,0:T(8,128)(2,1)} %proj.1, bf16[256,896]{1,0:T(8,128)(2,1)} %weight.1, f32[8,896]{1,0:T(8,128)} %moment.1, f32[8,896]{1,0:T(8,128)} %second.1), custom_call_target="tpu_custom_call" | custom-call | tf_op jit(solution)/shard_map/directions/pallas_call | solution.py:206
  36.5 0.8 %store.1 = (bf16[256,896]{1,0:T(8,128)(2,1)}, f32[8,896]{1,0:T(8,128)}, f32[8,896]{1,0:T(8,128)}) custom-call(bf16[256,896]{1,0:T(8,128)(2,1)S(1)} %get-tuple-element.5.weight, f32[2,8,896]{2,1,0:T(8,128)S(1)} %get-tuple-element.6.state), custom_call_target="tpu_custom_call" | custom-call | tf_op jit(solution)/shard_map/store/pallas_call | solution.py:245
